TPU v7x, 32 devices: a whole 2x2x4 slice. The times are simulated.
32 devices in a mesh: band: 8 (over z, y), grid: 4 (over x, core).
Axes of the slice: x: 2, y: 2, z: 4, core: 2. Of those that a mesh axis runs over, the one named last changes fastest.
Arguments:
- orbitals: bfloat16 [512, 64, 4096], P('band', 'grid'), may hold values from -6 to 6
- picks: int32 [1], replicated, may hold values from 0 to 511
Outputs:
- exchange_vectors: bfloat16 [512, 64, 4096], P('band', 'grid')
- gram: float32 [512, 512], P('band')
All inputs are finite; a program needn't handle non-finite values.
Results may differ from a plain program's by a relative error of at most 0.00085.
Values may be sent and summed in bfloat16 or wider, within the bound.
A program may use at most 192 MiB of HBM per device.

v0:
```python
import math
import jax
import jax.numpy as jnp
from jax import lax
from jax.sharding import PartitionSpec as P

NG = 64
NPTS = 262144
KERNEL_SCALE = 128.0
HIGHEST = lax.Precision.HIGHEST


def spread(value, axis, source):
    kept = jnp.where(lax.axis_index(axis) == source, value, 0).astype(value.dtype)
    return lax.psum(kept, axis)


def cas_matrix(length):
    products = (
        jnp.arange(length, dtype=jnp.int32)[:, None]
        * jnp.arange(length, dtype=jnp.int32)[None, :]
        % length
    )
    angles = products.astype(jnp.float32) * (2.0 * math.pi / length)
    return jnp.cos(angles) + jnp.sin(angles)


def folded_squares(first, length):
    frequency = first + jnp.arange(length, dtype=jnp.int32)
    folded = jnp.minimum(frequency, NG - frequency).astype(jnp.float32)
    return folded * folded


def transform_planes(field, matrix):
    batch, planes, square = field.shape
    shaped = field.reshape(batch, planes, NG, NG)
    shaped = jnp.einsum("bxyz,zk->bxyk", shaped, matrix, precision=HIGHEST)
    shaped = jnp.einsum("bxyz,yk->bxkz", shaped, matrix, precision=HIGHEST)
    return shaped.reshape(batch, planes, square)


def solve_potential(density):
    matrix = cas_matrix(NG)
    slab_rows = NG // lax.axis_size("grid")
    squares_first = folded_squares(0, NG)
    squares_second = folded_squares(lax.axis_index("grid") * slab_rows, slab_rows)
    summed = (
        squares_first[:, None, None] + squares_second[None, :, None] + squares_first[None, None, :]
    )
    table = jnp.where(summed > 0, KERNEL_SCALE / NPTS / jnp.maximum(summed, 1.0), 0.0)
    table = table.reshape(NG, slab_rows * NG)
    spectral = transform_planes(density, matrix)
    moved = jnp.einsum(
        "bxq,xk->bkq",
        lax.all_to_all(spectral, "grid", split_axis=2, concat_axis=1, tiled=True),
        matrix,
        precision=HIGHEST,
    )
    moved = moved * table[None]
    moved = jnp.einsum("bxq,xk->bkq", moved, matrix, precision=HIGHEST)
    slabs = lax.all_to_all(moved, "grid", split_axis=1, concat_axis=2, tiled=True)
    return transform_planes(slabs, matrix)


def apply_exchange(values, partners, solver):
    accumulated = jnp.zeros(values.shape, jnp.float32)
    partner = partners[0]
    potential = solver(values * partner[None])
    accumulated = accumulated - potential * partner[None]
    return accumulated.astype(jnp.bfloat16)


def per_device(orbitals, picks):
    local_bands = orbitals.shape[0]
    target = picks[0]
    owner = target // local_bands
    offset = target % local_bands
    mine = lax.dynamic_index_in_dim(orbitals, offset, 0, keepdims=False)
    partners = [spread(mine, "band", owner).astype(jnp.float32)]
    vectors = apply_exchange(orbitals.astype(jnp.float32), partners, solve_potential)
    flat_orbitals = orbitals.reshape(local_bands, -1)
    flat_vectors = vectors.reshape(local_bands, -1)
    spread_orbitals, spread_vectors = (
        lax.all_to_all(flat_orbitals, "band", split_axis=1, concat_axis=0, tiled=True),
        lax.all_to_all(flat_vectors, "band", split_axis=1, concat_axis=0, tiled=True),
    )
    product = lax.dot_general(
        spread_orbitals,
        spread_vectors,
        (((1,), (1,)), ((), ())),
        preferred_element_type=jnp.float32,
    )
    partial_rows = lax.psum_scatter(product * (1.0 / NPTS), "band", scatter_dimension=0, tiled=True)
    gram = lax.psum(partial_rows, "grid")
    return (vectors, gram)


def solution(mesh):
    return jax.shard_map(
        per_device,
        mesh=mesh,
        in_specs=(P("band", "grid", None), P()),
        out_specs=(P("band", "grid", None), P("band", None)),
        check_vma=False,
    )
```

profile of v0, /device:TPU:0, one launch (start us, length us, event | category | flops | bytes accessed | tf_op | source)
XLA Modules:
  0.0 1356.4 jit_solution(10697332559528059427)
XLA Ops:
  7.9 1.6 select_bitcast_fusion
  9.5 74.8 %all-reduce.3.cloned.1.call-done = bf16[16,4096]{1,0:T(8,128)(2,1)} async-done(((bf16[16,4096]{1,0:T(8,128)(2,1)}), bf16[16,4096]{1,0:T(8,128)(2,1)}) %all-reduce.3.cloned.1.call-update) | async-done | bytes 131088 | tf_op jit(solution)/shard_map/psum | solution.py:15
  84.3 0.9 convert_element_type.50
  85.2 0.7 copy-done
  85.9 11.5 convert_multiply_fusion
  97.4 27.0 %reshape.119 = f32[64,16,64,64]{3,2,1,0:T(8,128)} reshape(f32[64,16,4096]{2,1,0:T(8,128)} %convert_multiply_fusion) | data formatting | bytes 33554432 | tf_op jit(solution)/shard_map/reshape | solution.py:36
  124.4 33.2 %fusion.15 = f32[64,16,64,64]{3,2,1,0:T(8,128)} fusion(f32[64,16,64,64]{3,2,1,0:T(8,128)} %reshape.119), kind=kOutput, calls=%fused_computation.25 | convolution fusion | flops 3221286912 | bytes 33554432 | tf_op jit(solution)/shard_map/bxyz,zk->bxyk/dot_general | solution.py:37
  157.6 37.2 %convolution_bitcast_fusion.1 = f32[64,16,64,64]{3,2,1,0:T(8,128)} fusion(f32[64,16,64,64]{3,2,1,0:T(8,128)} %fusion.15), kind=kOutput, calls=%fused_computation.10 | convolution fusion | flops 3221286912 | bytes 33554432 | tf_op jit(solution)/shard_map/bxyz,yk->bxkz/dot_general | solution.py:38
  194.9 33.0 %copy.39 = f32[64,16,64,64]{0,1,3,2:T(8,128)} copy(f32[64,16,64,64]{3,2,1,0:T(8,128)} %convolution_bitcast_fusion.1) | data formatting | bytes 33554432 | tf_op jit(solution)/shard_map/reshape | solution.py:39
  227.9 42.5 %reshape.130 = f32[4,1,1048576]{2,1,0:T(1,128)} reshape(f32[4096,16,64]{2,1,0:T(8,128)} %bitcast.70) | data formatting | bytes 33554432
  270.4 7.0 all-to-all-start
  277.4 0.1 broadcast_add_fusion
  277.5 0.2 add.104
  277.7 0.2 add.105
  277.9 0.1 add.107
  278.0 0.1 divide_select_fusion
  278.0 182.4 %all-to-all-done = f32[4,1,1048576]{2,1,0:T(1,128)} async-done(((f32[4,1,1048576]{2,1,0:T(1,128)}), f32[4,1,1048576]{2,1,0:T(1,128)}, u32[]{:S(2)}, u32[]{:S(2)}) %all-to-all-start) | async-done | bytes 16777248 | tf_op jit(solution)/shard_map/all_to_all | solution.py:55
  460.5 0.5 broadcast.113
  461.0 54.2 %reduce = f32[4,1048576]{1,0:T(4,128)} reduce(f32[4,1,1048576]{2,1,0:T(1,128)} %all-to-all-done, f32[]{:T(128)} %broadcast.113), dimensions={1}, to_apply=%all_to_all.50.reduce_sub_computation | reduce | bytes 33554436 | tf_op jit(solution)/shard_map/all_to_all | solution.py:55
  515.2 55.1 %reshape.131 = f32[4096,16,64]{2,1,0:T(8,128)} reshape(f32[4,1048576]{1,0:T(4,128)} %reduce) | data formatting | bytes 33554432
  570.3 26.6 %copy.40 = f32[64,16,4,1024]{3,2,1,0:T(4,128)} copy(f32[64,16,4,1024]{0,1,3,2:T(8,128)} %bitcast.69) | data formatting | bytes 33554432 | tf_op jit(solution)/shard_map/all_to_all | solution.py:55
  596.9 20.4 %copy.28 = f32[64,4,16,1024]{3,2,1,0:T(8,128)} copy(f32[64,4,16,1024]{3,1,2,0:T(4,128)} %bitcast.71) | data formatting | bytes 33554432 | tf_op jit(solution)/shard_map/all_to_all | solution.py:55
  617.3 21.9 %fusion.20 = f32[64,64,1024]{2,0,1:T(8,128)} fusion(f32[64,64,1024]{2,1,0:T(8,128)} %bitcast.73), kind=kOutput, calls=%fused_computation.30 | convolution fusion | flops 3221286912 | bytes 33554432 | tf_op jit(solution)/shard_map/bxq,xk->bkq/dot_general | solution.py:53
  639.3 22.2 %fusion.5 = f32[64,64,1024]{2,1,0:T(8,128)} fusion(f32[64,64,1024]{2,0,1:T(8,128)} %fusion.20, f32[64,1024]{1,0:T(8,128)S(1)} %divide_select_fusion), kind=kOutput, calls=%fused_computation.11 | convolution fusion | flops 3225481216 | bytes 33816576 | tf_op jit(solution)/shard_map/bxq,xk->bkq/dot_general | solution.py:60
  661.5 17.7 %copy.29 = f32[64,64,1024]{2,0,1:T(8,128)} copy(f32[64,64,1024]{2,1,0:T(8,128)} %fusion.5) | data formatting | bytes 33554432 | tf_op jit(solution)/shard_map/bxq,xk->bkq/transpose | solution.py:60
  679.2 7.2 all-to-all-start.1
  686.4 13.0 all_to_all.60
  699.4 11.2 copy.33
  710.7 158.8 %all-to-all-done.1 = f32[64,64,1024]{2,0,1:T(8,128)} async-done(((f32[64,64,1024]{2,0,1:T(8,128)}), f32[64,64,1024]{2,0,1:T(8,128)}, u32[]{:S(2)}, u32[]{:S(2)}) %all-to-all-start.1) | async-done | bytes 16777248 | tf_op jit(solution)/shard_map/all_to_all | solution.py:61
  869.4 5.0 all-to-all-start.3
  874.5 0.0 reduce-scatter.4.cloned.1.call-start
  874.6 20.9 %copy.50 = f32[64,4,16,1024]{3,1,2,0:T(4,128)} copy(f32[64,4,16,1024]{3,0,2,1:T(8,128)} %bitcast.14) | data formatting | bytes 33554432 | tf_op jit(solution)/shard_map/all_to_all | solution.py:61
  895.4 27.6 %reshape.121 = f32[64,16,64,64]{3,2,1,0:T(8,128)} reshape(f32[64,16,4,1024]{3,2,1,0:T(4,128)} %bitcast.72) | data formatting | bytes 33554432 | tf_op jit(solution)/shard_map/reshape | solution.py:36
  923.0 33.2 %fusion.13 = f32[64,16,64,64]{3,2,1,0:T(8,128)} fusion(f32[64,16,64,64]{3,2,1,0:T(8,128)} %reshape.121), kind=kOutput, calls=%fused_computation.23 | convolution fusion | flops 3221286912 | bytes 33554432 | tf_op jit(solution)/shard_map/bxyz,zk->bxyk/dot_general | solution.py:37
  956.3 37.3 %convolution_bitcast_fusion = f32[64,16,64,64]{3,2,1,0:T(8,128)} fusion(f32[64,16,64,64]{3,2,1,0:T(8,128)} %fusion.13), kind=kOutput, calls=%fused_computation.9 | convolution fusion | flops 3221286912 | bytes 33554432 | tf_op jit(solution)/shard_map/bxyz,yk->bxkz/dot_general | solution.py:38
  993.6 27.9 %reshape.123 = f32[64,8,8192]{2,1,0:T(8,128)} reshape(f32[64,16,64,64]{3,2,1,0:T(8,128)} %convolution_bitcast_fusion) | data formatting | bytes 33554432 | tf_op jit(solution)/shard_map/reshape | solution.py:39
  1021.5 17.6 %fusion.3 = bf16[64,8,8192]{2,0,1:T(8,128)(2,1)} fusion(f32[64,8,8192]{2,1,0:T(8,128)} %reshape.123, f32[8,8192]{1,0:T(8,128)S(1)} %mul.138), kind=kLoop, calls=%fused_computation.4 | loop fusion | flops 12582912 | bytes 25427968 | tf_op jit(solution)/shard_map/convert_element_type | solution.py:70
  1039.1 18.5 %all-to-all-done.3 = bf16[64,8,8192]{2,0,1:T(8,128)(2,1)} async-done(((bf16[64,8,8192]{2,0,1:T(8,128)(2,1)}), bf16[64,8,8192]{2,0,1:T(8,128)(2,1)}, u32[]{:S(2)}, u32[]{:S(2)}) %all-to-all-start.3) | async-done | bytes 8388640 | tf_op jit(solution)/shard_map/all_to_all | solution.py:84
  1057.6 186.9 %all_to_all.68 = bf16[64,8,8192]{2,0,1:T(8,128)(2,1)S(1)} all-to-all(bf16[64,8,8192]{2,0,1:T(8,128)(2,1)} %fusion.3), channel_id=1, replica_groups=mesh['band'=8,'grid'=4] {'band'}, dimensions={1} | all-to-all | bytes 16777216 | tf_op jit(solution)/shard_map/all_to_all | solution.py:85
  1244.4 7.1 fusion.9
  1251.5 1.3 copy.42
  1252.9 0.0 all-reduce.5.cloned.1.call-start
  1252.9 28.0 %reshape.122 = f32[64,16,4096]{2,1,0:T(8,128)} reshape(f32[64,16,64,64]{3,2,1,0:T(8,128)} %convolution_bitcast_fusion) | data formatting | bytes 33554432 | tf_op jit(solution)/shard_map/reshape | solution.py:39
  1281.0 33.7 %reduce-scatter.4.cloned.1.call-done = f32[64,512]{1,0:T(8,128)} async-done(((f32[512,512]{1,0:T(8,128)}), f32[64,512]{1,0:T(8,128)}) %reduce-scatter.4.cloned.1.call-update) | async-done | bytes 131088
  1314.6 1.7 copy.43
  1316.4 9.5 subtract_convert_fusion
  1325.9 22.1 %all-reduce.5.cloned.1.call-done = f32[64,512]{0,1:T(8,128)} async-done(((f32[64,512]{0,1:T(8,128)}), f32[64,512]{0,1:T(8,128)}) %all-reduce.5.cloned.1.call-update) | async-done | bytes 131088 | tf_op jit(solution)/shard_map/psum | solution.py:94
  1348.0 1.7 copy.34
  (13 shorter events, 0.2 us)
Async XLA Ops:
  7.2 77.1 %all-reduce.3.cloned.1.call-start = ((), (), s32[]{:S(2)}) async-start(), calls=%async_computation.5 | async-start | bytes 262144 | tf_op jit(solution)/shard_map/psum | solution.py:15
  85.2 0.7 copy-start
  270.4 190.0 %all-to-all-start = ((f32[4,1,1048576]{2,1,0:T(1,128)}), f32[4,1,1048576]{2,1,0:T(1,128)}, u32[]{:S(2)}, u32[]{:S(2)}) async-start(f32[4,1,1048576]{2,1,0:T(1,128)} %reshape.130), calls=%async_computation | async-start | bytes 33554432 | tf_op jit(solution)/shard_map/all_to_all | solution.py:55
  679.2 190.2 %all-to-all-start.1 = ((f32[64,64,1024]{2,0,1:T(8,128)}), f32[64,64,1024]{2,0,1:T(8,128)}, u32[]{:S(2)}, u32[]{:S(2)}) async-start(f32[64,64,1024]{2,0,1:T(8,128)} %copy.29), calls=%async_computation.1 | async-start | bytes 33554432 | tf_op jit(solution)/shard_map/all_to_all | solution.py:61
  699.4 175.1 %copy-start.2 = (bf16[16,4096]{1,0:T(8,128)(2,1)S(1)}, bf16[16,4096]{1,0:T(8,128)(2,1)}, u32[]{:S(2)}) copy-start(bf16[16,4096]{1,0:T(8,128)(2,1)} %all-reduce.3.cloned.1.call-done) | copy-start | bytes 393220
  869.4 188.2 %all-to-all-start.3 = ((bf16[64,8,8192]{2,0,1:T(8,128)(2,1)}), bf16[64,8,8192]{2,0,1:T(8,128)(2,1)}, u32[]{:S(2)}, u32[]{:S(2)}) async-start(bf16[64,8,8192]{2,0,1:T(8,128)(2,1)} %copy.33), calls=%async_computation.3 | async-start | bytes 16777216 | tf_op jit(solution)/shard_map/all_to_all | solution.py:84
  874.5 440.2 %reduce-scatter.4.cloned.1.call-start = ((), (), s32[]{:S(2)}) async-start(), calls=%async_computation.7 | async-start | bytes 1179648
  1252.9 63.5 %copy-start.1 = (f32[16,4096]{1,0:T(8,128)S(1)}, f32[16,4096]{1,0:T(8,128)}, u32[]{:S(2)}) copy-start(f32[16,4096]{1,0:T(8,128)} %copy-done) | copy-start | bytes 786436
  1252.9 95.1 %all-reduce.5.cloned.1.call-start = ((), (), s32[]{:S(2)}) async-start(), calls=%async_computation.6 | async-start | bytes 524288 | tf_op jit(solution)/shard_map/psum | solution.py:94
Sparse Core Ops, SparseCore 0:
  11.9 72.3 all-reduce.2
  1253.0 61.5 reduce-scatter.3
  1317.0 30.9 all-reduce.4
where the time goes:
time: 1370 us; the launch traced here: 1360 us
  waiting for transfers between devices  490 us (36%)
  local copies, waits for them, and re-layouts  358 us (26%)
  matrix products  192 us (14%)
  blocking collectives  187 us (14%)
  other arithmetic  95.4 us (7%)
  starting transfers between devices  19.3 us (1%)
  between operations  14.7 us (1%)
    all_to_all x1, blocking collectives, per_device(): lax.all_to_all(flat_vectors, 'band', split_axis=1, concat_axis=0, tiled=T...  187 us
    all_to_all x1, waiting for transfers between devices, solve_potential(): lax.all_to_all(spectral, 'grid', split_axis=2, concat_axis=1, tiled=True)  182 us
    all_to_all x1, waiting for transfers between devices, solve_potential(): lax.all_to_all(moved, 'grid', split_axis=1, concat_axis=2, tiled=True)  159 us
    unnamed x11, local copies, waits for them, and re-layouts  103 us
    reshape x3, local copies, waits for them, and re-layouts, transform_planes(): return shaped.reshape(batch, planes, square)  89 us
    psum x1, waiting for transfers between devices, spread(): return lax.psum(kept, axis)  74.8 us
    dot_general x2, matrix products, transform_planes(): shaped = jnp.einsum('bxyz,yk->bxkz', shaped, matrix, precision=HIGHEST)  74.5 us
    dot_general x2, matrix products, transform_planes(): shaped = jnp.einsum('bxyz,zk->bxyk', shaped, matrix, precision=HIGHEST)  66.5 us
  transfers between devices with their start and end apart: 6, of which 6 were waited for; matrix products, arithmetic and copies ran while one was open for 16% of the time, Pallas kernels for 0%

commit v1 on v0

--- a/solution.py
+++ b/solution.py
@@ -52,7 +52,12 @@
     spectral = transform_planes(density, matrix)
     moved = jnp.einsum(
         "bxq,xk->bkq",
-        lax.all_to_all(spectral, "grid", split_axis=2, concat_axis=1, tiled=True),
+        jnp.concatenate(
+            lax.all_to_all(
+                jnp.stack(jnp.split(spectral, lax.axis_size("grid"), axis=2)), "grid", 0, 0
+            ),
+            axis=1,
+        ),
         matrix,
         precision=HIGHEST,
     )

time: 1370 us -> 1190 us (0.87)
  local copies, waits for them, and re-layouts: 358 us -> 226 us
  other arithmetic: 95.4 us -> 47.2 us
    unnamed x11 -> x9, local copies, waits for them, and re-layouts: 103 us -> 5.47 us
    all_to_all x1 -> x0, other arithmetic: 54.2 us -> none  [solve_potential(): lax.all_to_all(spectral, 'grid', split_axis=2, concat_axis=1, tiled=True)]
    all_to_all x3 -> x1, local copies, waits for them, and re-layouts: 47.5 us -> 11.8 us  [solve_potential(): lax.all_to_all(jnp.stack(jnp.split(spectral, lax.axis_size('grid'), axis=...]
  transfers between devices with their start and end apart: 6 -> 6, of which waited for: 6 -> 6; matrix products, arithmetic and copies ran while one was open for 16% -> 18% of each run, Pallas kernels for 0% -> 0%
where the time goes in v1:
time: 1190 us; the launch traced here: 1180 us
  waiting for transfers between devices  490 us (41%)
  local copies, waits for them, and re-layouts  226 us (19%)
  matrix products  192 us (16%)
  blocking collectives  187 us (16%)
  other arithmetic  47.2 us (4%)
  starting transfers between devices  19.8 us (2%)
  between operations  14.7 us (1%)
    all_to_all x1, blocking collectives, per_device(): lax.all_to_all(flat_vectors, 'band', split_axis=1, concat_axis=0, tiled=T...  187 us
    all_to_all x1, waiting for transfers between devices, solve_potential(): lax.all_to_all(jnp.stack(jnp.split(spectral, lax.axis_size('grid'), axis=...  182 us
    all_to_all x1, waiting for transfers between devices, solve_potential(): lax.all_to_all(moved, 'grid', split_axis=1, concat_axis=2, tiled=True)  159 us
    reshape x3, local copies, waits for them, and re-layouts, transform_planes(): return shaped.reshape(batch, planes, square)  83.9 us
    psum x1, waiting for transfers between devices, spread(): return lax.psum(kept, axis)  74.8 us
    dot_general x2, matrix products, transform_planes(): shaped = jnp.einsum('bxyz,yk->bxkz', shaped, matrix, precision=HIGHEST)  74.6 us
    dot_general x2, matrix products, transform_planes(): shaped = jnp.einsum('bxyz,zk->bxyk', shaped, matrix, precision=HIGHEST)  66.5 us
    reshape x2, local copies, waits for them, and re-layouts, transform_planes(): shaped = field.reshape(batch, planes, NG, NG)  54.6 us
  transfers between devices with their start and end apart: 6, of which 6 were waited for; matrix products, arithmetic and copies ran while one was open for 18% of the time, Pallas kernels for 0%

profile of v1, /device:TPU:0, one launch (start us, length us, event | category | flops | bytes accessed | tf_op | source)
XLA Modules:
  0.0 1177.0 jit_solution(468874242345907901)
XLA Ops:
  7.2 0.0 all-reduce.3.cloned.1.call-start
  7.9 1.6 select_bitcast_fusion
  9.5 0.0 all-reduce.3.cloned.1.call-update
  9.5 74.8 %all-reduce.3.cloned.1.call-done = bf16[16,4096]{1,0:T(8,128)(2,1)} async-done(((bf16[16,4096]{1,0:T(8,128)(2,1)}), bf16[16,4096]{1,0:T(8,128)(2,1)}) %all-reduce.3.cloned.1.call-update) | async-done | bytes 131088 | tf_op jit(solution)/shard_map/psum | solution.py:15
  84.3 0.9 convert_element_type.50
  85.2 0.7 copy-done
  85.9 11.5 convert_multiply_fusion
  97.4 27.0 %reshape.125 = f32[64,16,64,64]{3,2,1,0:T(8,128)} reshape(f32[64,16,4096]{2,1,0:T(8,128)} %convert_multiply_fusion) | data formatting | bytes 33554432 | tf_op jit(solution)/shard_map/reshape | solution.py:36
  124.4 33.3 %fusion.15 = f32[64,16,64,64]{3,2,1,0:T(8,128)} fusion(f32[64,16,64,64]{3,2,1,0:T(8,128)} %reshape.125), kind=kOutput, calls=%fused_computation.30 | convolution fusion | flops 3221286912 | bytes 33554432 | tf_op jit(solution)/shard_map/bxyz,zk->bxyk/dot_general | solution.py:37
  157.7 37.2 %convolution_bitcast_fusion.1 = f32[64,16,64,64]{3,2,1,0:T(8,128)} fusion(f32[64,16,64,64]{3,2,1,0:T(8,128)} %fusion.15), kind=kOutput, calls=%fused_computation.11 | convolution fusion | flops 3221286912 | bytes 33554432 | tf_op jit(solution)/shard_map/bxyz,yk->bxkz/dot_general | solution.py:38
  194.9 27.9 %reshape.126 = f32[64,16,4096]{2,1,0:T(8,128)} reshape(f32[64,16,64,64]{3,2,1,0:T(8,128)} %convolution_bitcast_fusion.1) | data formatting | bytes 33554432 | tf_op jit(solution)/shard_map/reshape | solution.py:39
  222.8 6.7 slice_bitcast_fusion.3
  229.6 6.0 pad_maximum_fusion
  235.6 7.5 all-to-all-start
  243.1 0.1 broadcast_add_fusion
  243.2 0.2 add.104
  243.4 0.2 add.105
  243.6 0.1 add.107
  243.7 0.1 divide_select_fusion
  243.7 182.4 %all-to-all-done = f32[4,64,16,1024]{3,2,1,0:T(8,128)} async-done(((f32[4,64,16,1024]{3,2,1,0:T(8,128)}), f32[4,64,16,1024]{3,2,1,0:T(8,128)}, u32[]{:S(2)}, u32[]{:S(2)}) %all-to-all-start) | async-done | bytes 16777248 | tf_op jit(solution)/shard_map/all_to_all | solution.py:56
  426.2 11.8 %copy.21 = f32[4,64,16,1024]{3,2,0,1:T(8,128)} copy(f32[4,64,16,1024]{3,2,1,0:T(8,128)} %all-to-all-done) | data formatting | bytes 33554432 | tf_op jit(solution)/shard_map/all_to_all | solution.py:56
  438.0 21.8 %fusion.20 = f32[64,64,1024]{2,0,1:T(8,128)} fusion(f32[64,64,1024]{2,1,0:T(8,128)} %bitcast.77), kind=kOutput, calls=%fused_computation.35 | convolution fusion | flops 3221286912 | bytes 33554432 | tf_op jit(solution)/shard_map/bxq,xk->bkq/dot_general | solution.py:53
  459.7 22.4 %fusion.5 = f32[64,64,1024]{2,1,0:T(8,128)} fusion(f32[64,64,1024]{2,0,1:T(8,128)} %fusion.20, f32[64,1024]{1,0:T(8,128)S(1)} %divide_select_fusion), kind=kOutput, calls=%fused_computation.12 | convolution fusion | flops 3225481216 | bytes 33816576 | tf_op jit(solution)/shard_map/bxq,xk->bkq/dot_general | solution.py:65
  482.1 17.7 %copy.22 = f32[64,64,1024]{2,0,1:T(8,128)} copy(f32[64,64,1024]{2,1,0:T(8,128)} %fusion.5) | data formatting | bytes 33554432 | tf_op jit(solution)/shard_map/bxq,xk->bkq/transpose | solution.py:65
  499.8 7.2 all-to-all-start.1
  507.0 13.0 %all_to_all.47 = bf16[64,8,8192]{2,1,0:T(8,128)(2,1)} reshape(bf16[64,16,4096]{2,1,0:T(8,128)(2,1)} %param.2) | data formatting | bytes 16777216 | tf_op jit(solution)/shard_map/all_to_all | solution.py:89
  520.1 11.2 copy.26
  531.3 158.8 %all-to-all-done.1 = f32[64,64,1024]{2,0,1:T(8,128)} async-done(((f32[64,64,1024]{2,0,1:T(8,128)}), f32[64,64,1024]{2,0,1:T(8,128)}, u32[]{:S(2)}, u32[]{:S(2)}) %all-to-all-start.1) | async-done | bytes 16777248 | tf_op jit(solution)/shard_map/all_to_all | solution.py:66
  690.1 5.0 all-to-all-start.3
  695.1 0.0 reduce-scatter.4.cloned.1.call-start
  695.2 20.9 %copy.41 = f32[64,4,16,1024]{3,1,2,0:T(4,128)} copy(f32[64,4,16,1024]{3,0,2,1:T(8,128)} %bitcast.16) | data formatting | bytes 33554432 | tf_op jit(solution)/shard_map/all_to_all | solution.py:66
  716.1 27.6 %reshape.129 = f32[64,16,64,64]{3,2,1,0:T(8,128)} reshape(f32[64,16,4,1024]{3,2,1,0:T(4,128)} %bitcast.76) | data formatting | bytes 33554432 | tf_op jit(solution)/shard_map/reshape | solution.py:36
  743.7 33.3 %fusion.13 = f32[64,16,64,64]{3,2,1,0:T(8,128)} fusion(f32[64,16,64,64]{3,2,1,0:T(8,128)} %reshape.129), kind=kOutput, calls=%fused_computation.28 | convolution fusion | flops 3221286912 | bytes 33554432 | tf_op jit(solution)/shard_map/bxyz,zk->bxyk/dot_general | solution.py:37
  776.9 37.3 %convolution_bitcast_fusion = f32[64,16,64,64]{3,2,1,0:T(8,128)} fusion(f32[64,16,64,64]{3,2,1,0:T(8,128)} %fusion.13), kind=kOutput, calls=%fused_computation.10 | convolution fusion | flops 3221286912 | bytes 33554432 | tf_op jit(solution)/shard_map/bxyz,yk->bxkz/dot_general | solution.py:38
  814.2 27.9 %reshape.131 = f32[64,8,8192]{2,1,0:T(8,128)} reshape(f32[64,16,64,64]{3,2,1,0:T(8,128)} %convolution_bitcast_fusion) | data formatting | bytes 33554432 | tf_op jit(solution)/shard_map/reshape | solution.py:39
  842.2 17.6 %fusion.3 = bf16[64,8,8192]{2,0,1:T(8,128)(2,1)} fusion(f32[64,8,8192]{2,1,0:T(8,128)} %reshape.131, f32[8,8192]{1,0:T(8,128)S(1)} %mul.138), kind=kLoop, calls=%fused_computation.5 | loop fusion | flops 12582912 | bytes 25427968 | tf_op jit(solution)/shard_map/convert_element_type | solution.py:75
  859.7 18.5 %all-to-all-done.3 = bf16[64,8,8192]{2,0,1:T(8,128)(2,1)} async-done(((bf16[64,8,8192]{2,0,1:T(8,128)(2,1)}), bf16[64,8,8192]{2,0,1:T(8,128)(2,1)}, u32[]{:S(2)}, u32[]{:S(2)}) %all-to-all-start.3) | async-done | bytes 8388640 | tf_op jit(solution)/shard_map/all_to_all | solution.py:89
  878.2 186.9 %all_to_all.55 = bf16[64,8,8192]{2,0,1:T(8,128)(2,1)S(1)} all-to-all(bf16[64,8,8192]{2,0,1:T(8,128)(2,1)} %fusion.3), channel_id=1, replica_groups=mesh['band'=8,'grid'=4] {'band'}, dimensions={1} | all-to-all | bytes 16777216 | tf_op jit(solution)/shard_map/all_to_all | solution.py:90
  1065.1 7.1 fusion.9
  1072.2 1.3 copy.33
  1073.5 0.0 reduce-scatter.4.cloned.1.call-update
  1073.5 0.0 all-reduce.5.cloned.1.call-start
  1073.6 28.0 %reshape.130 = f32[64,16,4096]{2,1,0:T(8,128)} reshape(f32[64,16,64,64]{3,2,1,0:T(8,128)} %convolution_bitcast_fusion) | data formatting | bytes 33554432 | tf_op jit(solution)/shard_map/reshape | solution.py:39
  1101.6 33.6 %reduce-scatter.4.cloned.1.call-done = f32[64,512]{1,0:T(8,128)} async-done(((f32[512,512]{1,0:T(8,128)}), f32[64,512]{1,0:T(8,128)}) %reduce-scatter.4.cloned.1.call-update) | async-done | bytes 131088
  1135.2 1.7 copy.34
  1137.0 9.5 subtract_convert_fusion
  1146.5 22.1 %all-reduce.5.cloned.1.call-done = f32[64,512]{0,1:T(8,128)} async-done(((f32[64,512]{0,1:T(8,128)}), f32[64,512]{0,1:T(8,128)}) %all-reduce.5.cloned.1.call-update) | async-done | bytes 131088 | tf_op jit(solution)/shard_map/psum | solution.py:99
  1168.6 1.7 copy.27
  (10 shorter events, 0.1 us)
Async XLA Ops:
  7.2 77.1 %all-reduce.3.cloned.1.call-start = ((), (), s32[]{:S(2)}) async-start(), calls=%async_computation.5 | async-start | bytes 262144 | tf_op jit(solution)/shard_map/psum | solution.py:15
  85.2 0.7 copy-start
  235.6 190.6 %all-to-all-start = ((f32[4,64,16,1024]{3,2,1,0:T(8,128)}), f32[4,64,16,1024]{3,2,1,0:T(8,128)}, u32[]{:S(2)}, u32[]{:S(2)}) async-start(f32[4,64,16,1024]{3,2,1,0:T(8,128)} %pad_maximum_fusion), calls=%async_computation | async-start | bytes 33554432 | tf_op jit(solution)/shard_map/all_to_all | solution.py:56
  499.8 190.2 %all-to-all-start.1 = ((f32[64,64,1024]{2,0,1:T(8,128)}), f32[64,64,1024]{2,0,1:T(8,128)}, u32[]{:S(2)}, u32[]{:S(2)}) async-start(f32[64,64,1024]{2,0,1:T(8,128)} %copy.22), calls=%async_computation.1 | async-start | bytes 33554432 | tf_op jit(solution)/shard_map/all_to_all | solution.py:66
  520.1 175.1 %copy-start.2 = (bf16[16,4096]{1,0:T(8,128)(2,1)S(1)}, bf16[16,4096]{1,0:T(8,128)(2,1)}, u32[]{:S(2)}) copy-start(bf16[16,4096]{1,0:T(8,128)(2,1)} %all-reduce.3.cloned.1.call-done) | copy-start | bytes 393220
  690.1 188.2 %all-to-all-start.3 = ((bf16[64,8,8192]{2,0,1:T(8,128)(2,1)}), bf16[64,8,8192]{2,0,1:T(8,128)(2,1)}, u32[]{:S(2)}, u32[]{:S(2)}) async-start(bf16[64,8,8192]{2,0,1:T(8,128)(2,1)} %copy.26), calls=%async_computation.3 | async-start | bytes 16777216 | tf_op jit(solution)/shard_map/all_to_all | solution.py:89
  695.1 440.1 %reduce-scatter.4.cloned.1.call-start = ((), (), s32[]{:S(2)}) async-start(), calls=%async_computation.7 | async-start | bytes 1179648
  1073.5 63.5 %copy-start.1 = (f32[16,4096]{1,0:T(8,128)S(1)}, f32[16,4096]{1,0:T(8,128)}, u32[]{:S(2)}) copy-start(f32[16,4096]{1,0:T(8,128)} %copy-done) | copy-start | bytes 786436
  1073.5 95.1 %all-reduce.5.cloned.1.call-start = ((), (), s32[]{:S(2)}) async-start(), calls=%async_computation.6 | async-start | bytes 524288 | tf_op jit(solution)/shard_map/psum | solution.py:99
Sparse Core Ops, SparseCore 0:
  11.9 72.3 all-reduce.2
  1073.6 61.5 reduce-scatter.3
  1137.5 30.9 all-reduce.4
